TPU v7x, 32 devices: a whole 2x2x4 slice. The times are simulated.
32 devices in a mesh: pts: 32 (over z, y, x, core).
Axes of the slice: x: 2, y: 2, z: 4, core: 2. Of those that a mesh axis runs over, the one named last changes fastest.
Arguments:
- features: bfloat16 [131072, 256], P('pts'), may hold values from -6 to 6
- coords: float32 [2, 131072], P(None, 'pts'), may hold values from 0 to 1
- fourier_basis: float32 [2, 64], replicated, may hold values from -4 to 4
- block_items: int32 [1024], P('pts'), may hold values from 0 to 15, as said below
- point_mask: int32 [131072], P('pts'), may hold values from 0 to 1, as said below
- cotangent: bfloat16 [131072, 256], P('pts'), may hold values from -6 to 6
- square_weight: float32 [7, 65536], P(None, 'pts')
- square_first: float32 [7, 65536], P(None, 'pts'), may hold values from -0.00061035156 to 0.00061035156
- square_second: float32 [7, 65536], P(None, 'pts'), may hold values from 2.5518217e-08 to 4.1221733e-07
- expand_weight: float32 [2, 131072], P(None, 'pts'), may hold values from -0.375 to 0.375
- expand_first: float32 [2, 131072], P(None, 'pts'), may hold values from -0.00061035156 to 0.00061035156
- expand_second: float32 [2, 131072], P(None, 'pts'), may hold values from 2.5518217e-08 to 4.1221733e-07
- contract_weight: float32 [2, 131072], P(None, 'pts'), may hold values from -0.25 to 0.25
- contract_first: float32 [2, 131072], P(None, 'pts'), may hold values from -0.00061035156 to 0.00061035156
- contract_second: float32 [2, 131072], P(None, 'pts'), may hold values from 2.5518217e-08 to 4.1221733e-07
- fourier_weight: float32 [32768], P('pts'), may hold values from -0.5 to 0.5
- fourier_first: float32 [32768], P('pts'), may hold values from -0.00061035156 to 0.00061035156
- fourier_second: float32 [32768], P('pts'), may hold values from 2.5518217e-08 to 4.1221733e-07
- vector_weight: float32 [8, 256], replicated
- vector_first: float32 [8, 256], replicated, may hold values from -0.001953125 to 0.001953125
- vector_second: float32 [8, 256], replicated, may hold values from 2.3555276e-07 to 3.7295854e-06
- hidden_weight: float32 [2, 512], replicated, may hold values from -1.8 to 1.8
- hidden_first: float32 [2, 512], replicated, may hold values from -0.001953125 to 0.001953125
- hidden_second: float32 [2, 512], replicated, may hold values from 7.361024e-09 to 1.1777638e-07
Outputs:
- layer_output: bfloat16 [131072, 256], P('pts')
- input_grad: float32 [131072, 256], P('pts')
- grad_norm: float32 [], replicated
- new_square_first: float32 [7, 65536], P(None, 'pts')
- new_square_second: float32 [7, 65536], P(None, 'pts')
- new_square_weight: float32 [7, 65536], P(None, 'pts')
- new_expand_first: float32 [2, 131072], P(None, 'pts')
- new_expand_second: float32 [2, 131072], P(None, 'pts')
- new_expand_weight: float32 [2, 131072], P(None, 'pts')
- new_contract_first: float32 [2, 131072], P(None, 'pts')
- new_contract_second: float32 [2, 131072], P(None, 'pts')
- new_contract_weight: float32 [2, 131072], P(None, 'pts')
- new_fourier_first: float32 [32768], P('pts')
- new_fourier_second: float32 [32768], P('pts')
- new_fourier_weight: float32 [32768], P('pts')
- new_vector_first: float32 [8, 256], replicated
- new_vector_second: float32 [8, 256], replicated
- new_vector_weight: float32 [8, 256], replicated
- new_hidden_first: float32 [2, 512], replicated
- new_hidden_second: float32 [2, 512], replicated
- new_hidden_weight: float32 [2, 512], replicated
Inputs may be any that keep to these rules, and one draw needn't show every extreme that they name: `block_items`: each of the 16 items owns two or more blocks of 128 points; the item of the first block also owns the last block. `point_mask`: the first point of every block of 128 points is 1.
All inputs are finite; a program needn't handle non-finite values.
Results may differ from a plain program's by a relative error of at most 0.02.
Values may be sent and summed in bfloat16 or wider, within the bound.
A program may use at most 192 MiB of HBM per device.

v0:
```python
import functools
import math
import types

import jax
import jax.numpy as jnp
from jax import lax
from jax.experimental import pallas as pl
from jax.experimental.pallas import tpu as pltpu
from jax.sharding import PartitionSpec as P

H = 8
E = 32
F = 512
FOUR = 128
BLOCK = 128
ITEM_PTS = 8192
STEP = 10


NORM_EPS = 1e-05
GELU_C = math.sqrt(2.0 / math.pi)
GELU_A = 0.044715
BETA_ONE = 0.9
BETA_TWO = 0.95
ADAM_EPS = 1e-08
WEIGHT_DECAY = 0.1
RATE_MATRIX = 0.05
RATE_VECTOR = 0.25
CLIP_NORM = 1.0
HIGHEST_PRECISION = lax.Precision.HIGHEST


def matmul(left, right):
    return jnp.dot(left, right, preferred_element_type=jnp.float32)


def matmul_left(left, right):
    return lax.dot_general(
        left, right, (((0,), (0,)), ((), ())), preferred_element_type=jnp.float32
    )


def matmul_right(left, right):
    return lax.dot_general(
        left, right, (((1,), (1,)), ((), ())), preferred_element_type=jnp.float32
    )


def gelu(values):
    return 0.5 * values * (1.0 + jnp.tanh(GELU_C * (values + GELU_A * values * values * values)))


def gelu_slope(values):
    tangent = jnp.tanh(GELU_C * (values + GELU_A * values * values * values))
    return 0.5 * (1.0 + tangent) + 0.5 * values * (1.0 - tangent * tangent) * GELU_C * (
        1.0 + 3.0 * GELU_A * values * values
    )


def norm_parts(values, norm_gain, norm_bias):
    centred = values - jnp.mean(values, axis=-1, keepdims=True)
    variance = jnp.mean(centred * centred, axis=-1, keepdims=True)
    root_inv = lax.rsqrt(variance + NORM_EPS)
    scaled = centred * root_inv
    return (scaled * norm_gain + norm_bias, scaled, root_inv)


def norm_back(upstream, scaled, root_inv, norm_gain):
    through = upstream * norm_gain
    centre = jnp.mean(through, axis=-1, keepdims=True)
    along = jnp.mean(through * scaled, axis=-1, keepdims=True)
    return root_inv * (through - centre - scaled * along)


def rotary_tables(coords):
    quarter = E // 4
    frequency = math.pi * (jnp.arange(quarter, dtype=jnp.float32) + 1.0) / quarter
    first_angle = coords[0][:, None] * frequency[None, :]
    second_angle = coords[1][:, None] * frequency[None, :]
    angles = jnp.concatenate([first_angle, first_angle, second_angle, second_angle], axis=1)
    return (jnp.cos(angles), jnp.sin(angles))


def rotate(values, cosine, sine):
    quarter = E // 4
    swapped = jnp.concatenate(
        [
            -values[..., quarter : 2 * quarter],
            values[..., :quarter],
            -values[..., 3 * quarter :],
            values[..., 2 * quarter : 3 * quarter],
        ],
        axis=-1,
    )
    return values * cosine[:, None, :] + swapped * sine[:, None, :]


def rotate_back(grads, cosine, sine):
    quarter = E // 4
    scaled = grads * sine[:, None, :]
    swapped = jnp.concatenate(
        [
            scaled[..., quarter : 2 * quarter],
            -scaled[..., :quarter],
            scaled[..., 3 * quarter :],
            -scaled[..., 2 * quarter : 3 * quarter],
        ],
        axis=-1,
    )
    return grads * cosine[:, None, :] + swapped


def fourier_features(coords, fourier_basis):
    phases = (
        2.0
        * math.pi
        * (
            coords[0][:, None] * fourier_basis[0][None, :]
            + coords[1][:, None] * fourier_basis[1][None, :]
        )
    )
    return jnp.concatenate([jnp.cos(phases), jnp.sin(phases)], axis=1)


def block_table(left, right, onehot):
    blocks = onehot.shape[0]
    per_block = jnp.einsum(
        "bphe,bphf->bhef",
        left.reshape(blocks, BLOCK, H, E),
        right.reshape(blocks, BLOCK, H, E),
        preferred_element_type=jnp.float32,
    )
    return jnp.einsum("ba,bhef->ahef", onehot, per_block, precision=HIGHEST_PRECISION)


def scale_round(table, inverse_count):
    return (table * inverse_count[:, None, None, None]).astype(jnp.bfloat16)


def spread(summary, onehot):
    selected = jnp.einsum(
        "ba,ahef->bhef", onehot.astype(jnp.bfloat16), summary, preferred_element_type=jnp.float32
    )
    return selected.astype(jnp.bfloat16)


def apply_summary(rows_low, block_summary, transposed):
    blocks = block_summary.shape[0]
    pattern = "bphf,bhef->bphe" if transposed else "bphe,bhef->bphf"
    mixed = jnp.einsum(
        pattern,
        rows_low.reshape(blocks, BLOCK, H, E),
        block_summary,
        preferred_element_type=jnp.float32,
    )
    return mixed.reshape(-1, H * E)


def galerkin_backward(
    grad_low, queries_low, keys_masked, values_low, block_summary, onehot, mask_float, reducer
):
    grad_masked = grad_low * mask_float.astype(jnp.bfloat16)
    grad_queries = apply_summary(grad_masked, block_summary, True)
    summary_grad = reducer(block_table(queries_low, grad_masked, onehot))
    block_grad = spread(summary_grad, onehot)
    grad_keys = apply_summary(values_low, block_grad, True) * mask_float
    grad_values = apply_summary(keys_masked, block_grad, False)
    return (grad_queries, grad_keys, grad_values)


def adam_update(weight, first, second, grad, factor, rate):
    clipped = grad * factor
    new_first = BETA_ONE * first + (1.0 - BETA_ONE) * clipped
    new_second = BETA_TWO * second + (1.0 - BETA_TWO) * clipped * clipped
    first_hat = new_first / (1.0 - BETA_ONE**STEP)
    second_hat = new_second / (1.0 - BETA_TWO**STEP)
    new_weight = weight - rate * (
        first_hat / (jnp.sqrt(second_hat) + ADAM_EPS) + WEIGHT_DECAY * weight
    )
    return (new_first, new_second, new_weight)


def own_share(full, width, along, start_index):
    return lax.dynamic_slice_in_dim(full, start_index * width, width, along)


def plain(
    features,
    coords,
    fourier_basis,
    block_items,
    point_mask,
    cotangent,
    square_weight,
    square_first,
    square_second,
    expand_weight,
    expand_first,
    expand_second,
    contract_weight,
    contract_first,
    contract_second,
    fourier_weight,
    fourier_first,
    fourier_second,
    vector_weight,
    vector_first,
    vector_second,
    hidden_weight,
    hidden_first,
    hidden_second,
):
    rows = features.shape[0]
    width = features.shape[1]
    blocks = rows // BLOCK
    devices = lax.axis_size("pts")
    items_total = rows * devices // ITEM_PTS
    gathered = (
        lax.all_gather(square_weight.astype(jnp.bfloat16), "pts", axis=1, tiled=True),
        lax.all_gather(expand_weight.astype(jnp.bfloat16), "pts", axis=1, tiled=True),
        lax.all_gather(contract_weight.astype(jnp.bfloat16), "pts", axis=1, tiled=True),
        lax.all_gather(fourier_weight.astype(jnp.bfloat16), "pts", axis=0, tiled=True),
    )
    square_full = gathered[0].reshape(7, width, width)
    expand_full = gathered[1].reshape(2, width, F)
    contract_full = gathered[2].reshape(2, F, width)
    fourier_full = gathered[3].reshape(FOUR, width)
    onehot = (block_items[:, None] == jnp.arange(items_total, dtype=jnp.int32)[None, :]).astype(
        jnp.float32
    )
    mask_float = point_mask.astype(jnp.float32)[:, None]
    mask_low = mask_float.astype(jnp.bfloat16)
    block_count = jnp.sum(mask_float.reshape(blocks, BLOCK), axis=1)
    local_count = jnp.dot(block_count, onehot, precision=HIGHEST_PRECISION)
    cosine, sine = rotary_tables(coords)
    phase_low = fourier_features(coords, fourier_basis).astype(jnp.bfloat16)
    inputs = features.astype(jnp.float32)
    normed, scaled_one, root_one = norm_parts(inputs, vector_weight[0], vector_weight[1])
    normed_low = normed.astype(jnp.bfloat16)
    joint_weight = jnp.concatenate([square_full[0], square_full[1], square_full[2]], axis=1)
    projected = matmul(normed_low, joint_weight)
    queries_low = (
        rotate(projected[:, :width].reshape(rows, H, E), cosine, sine)
        .reshape(rows, width)
        .astype(jnp.bfloat16)
    )
    keys_low = (
        rotate(projected[:, width : 2 * width].reshape(rows, H, E), cosine, sine)
        .reshape(rows, width)
        .astype(jnp.bfloat16)
    )
    keys_masked = keys_low * mask_low
    values_low = projected[:, 2 * width :].astype(jnp.bfloat16)
    self_local = block_table(keys_masked, values_low, onehot)
    self_table, item_count = lax.psum((self_local, local_count), "pts")
    inverse_count = 1.0 / item_count
    self_items = scale_round(self_table, inverse_count)
    self_summary = spread(self_items, onehot)
    attended_low = (apply_summary(queries_low, self_summary, False) * mask_float).astype(
        jnp.bfloat16
    )
    first_sum = inputs + matmul(attended_low, square_full[3])
    normed_mid, scaled_two, root_two = norm_parts(first_sum, vector_weight[2], vector_weight[3])
    middle_low = normed_mid.astype(jnp.bfloat16)
    hidden_pre = matmul(middle_low, expand_full[0]) + hidden_weight[0]
    hidden_low = gelu(hidden_pre).astype(jnp.bfloat16)
    encoded = first_sum + matmul(hidden_low, contract_full[0]) + vector_weight[6]
    normed_out, scaled_three, root_three = norm_parts(encoded, vector_weight[4], vector_weight[5])
    outer_low = normed_out.astype(jnp.bfloat16)
    pair_weight = jnp.concatenate([square_full[4], square_full[5]], axis=1)
    cross_projected = matmul(outer_low, pair_weight)
    cross_keys = cross_projected[:, :width].astype(jnp.bfloat16) * mask_low
    cross_values = cross_projected[:, width:].astype(jnp.bfloat16)
    cross_queries = matmul(phase_low, fourier_full).astype(jnp.bfloat16)
    cross_local = block_table(cross_keys, cross_values, onehot)
    cross_items = scale_round(lax.psum(cross_local, "pts"), inverse_count)
    cross_summary = spread(cross_items, onehot)
    decoded_low = (apply_summary(cross_queries, cross_summary, False) * mask_float).astype(
        jnp.bfloat16
    )
    latent = matmul(decoded_low, square_full[6])
    latent_low = latent.astype(jnp.bfloat16)
    spread_pre = matmul(latent_low, expand_full[1]) + hidden_weight[1]
    spread_low = gelu(spread_pre).astype(jnp.bfloat16)
    output = latent + matmul(spread_low, contract_full[1]) + vector_weight[7]
    cross_reducer = lambda table_part: scale_round(lax.psum(table_part, "pts"), inverse_count)
    self_reducer = lambda table_part: scale_round(lax.psum(table_part, "pts"), inverse_count)
    grad_output = cotangent.astype(jnp.float32)
    grad_bias_end = jnp.sum(grad_output, axis=0)
    grad_contract_spread = matmul_left(spread_low, cotangent)
    grad_spread = matmul_right(cotangent, contract_full[1]) * gelu_slope(spread_pre)
    grad_hidden_spread = jnp.sum(grad_spread, axis=0)
    grad_spread_low = grad_spread.astype(jnp.bfloat16)
    grad_expand_spread = matmul_left(latent_low, grad_spread_low)
    grad_latent = (grad_output + matmul_right(grad_spread_low, expand_full[1])).astype(jnp.bfloat16)
    grad_out_cross = matmul_left(decoded_low, grad_latent)
    grad_decoded = matmul_right(grad_latent, square_full[6]).astype(jnp.bfloat16)
    cross_back = galerkin_backward(
        grad_decoded,
        cross_queries,
        cross_keys,
        cross_values,
        cross_summary,
        onehot,
        mask_float,
        cross_reducer,
    )
    grad_fourier_full = matmul_left(phase_low, cross_back[0].astype(jnp.bfloat16))
    grad_pair_low = jnp.concatenate([cross_back[1], cross_back[2]], axis=1).astype(jnp.bfloat16)
    grad_pair_full = matmul_left(outer_low, grad_pair_low)
    grad_normed_out = matmul_right(grad_pair_low, pair_weight)
    grad_gain_three = jnp.sum(grad_normed_out * scaled_three, axis=0)
    grad_bias_three = jnp.sum(grad_normed_out, axis=0)
    grad_encoded = norm_back(grad_normed_out, scaled_three, root_three, vector_weight[4])
    grad_bias_middle = jnp.sum(grad_encoded, axis=0)
    grad_encoded_low = grad_encoded.astype(jnp.bfloat16)
    grad_contract_enc = matmul_left(hidden_low, grad_encoded_low)
    grad_hidden = matmul_right(grad_encoded_low, contract_full[0]) * gelu_slope(hidden_pre)
    grad_hidden_enc = jnp.sum(grad_hidden, axis=0)
    grad_hidden_low = grad_hidden.astype(jnp.bfloat16)
    grad_expand_enc = matmul_left(middle_low, grad_hidden_low)
    grad_middle = matmul_right(grad_hidden_low, expand_full[0])
    grad_gain_two = jnp.sum(grad_middle * scaled_two, axis=0)
    grad_bias_two = jnp.sum(grad_middle, axis=0)
    grad_first = grad_encoded + norm_back(grad_middle, scaled_two, root_two, vector_weight[2])
    grad_first_low = grad_first.astype(jnp.bfloat16)
    grad_out_self = matmul_left(attended_low, grad_first_low)
    grad_attended = matmul_right(grad_first_low, square_full[3]).astype(jnp.bfloat16)
    self_back = galerkin_backward(
        grad_attended,
        queries_low,
        keys_masked,
        values_low,
        self_summary,
        onehot,
        mask_float,
        self_reducer,
    )
    grad_queries = rotate_back(self_back[0].reshape(rows, H, E), cosine, sine).reshape(rows, width)
    grad_keys = rotate_back(self_back[1].reshape(rows, H, E), cosine, sine).reshape(rows, width)
    grad_joint_low = jnp.concatenate([grad_queries, grad_keys, self_back[2]], axis=1).astype(
        jnp.bfloat16
    )
    grad_joint_full = matmul_left(normed_low, grad_joint_low)
    grad_normed = matmul_right(grad_joint_low, joint_weight)
    grad_gain_one = jnp.sum(grad_normed * scaled_one, axis=0)
    grad_bias_one = jnp.sum(grad_normed, axis=0)
    grad_inputs = grad_first + norm_back(grad_normed, scaled_one, root_one, vector_weight[0])
    grad_square = jnp.stack(
        [
            grad_joint_full[:, :width],
            grad_joint_full[:, width : 2 * width],
            grad_joint_full[:, 2 * width :],
            grad_out_self,
            grad_pair_full[:, :width],
            grad_pair_full[:, width:],
            grad_out_cross,
        ]
    ).reshape(7, width * width)
    grad_expand = jnp.stack([grad_expand_enc, grad_expand_spread]).reshape(2, width * F)
    grad_contract = jnp.stack([grad_contract_enc, grad_contract_spread]).reshape(2, F * width)
    grad_fourier = grad_fourier_full.reshape(FOUR * width)
    grad_vector = jnp.stack(
        [
            grad_gain_one,
            grad_bias_one,
            grad_gain_two,
            grad_bias_two,
            grad_gain_three,
            grad_bias_three,
            grad_bias_middle,
            grad_bias_end,
        ]
    )
    grad_hidden_rows = jnp.stack([grad_hidden_enc, grad_hidden_spread])
    totals = lax.psum(
        (grad_square, grad_expand, grad_contract, grad_fourier, grad_vector, grad_hidden_rows),
        "pts",
    )
    squares = sum((jnp.sum(total_part * total_part) for total_part in totals))
    start_index = lax.axis_index("pts")
    share_square = own_share(totals[0], square_weight.shape[1], 1, start_index)
    share_expand = own_share(totals[1], expand_weight.shape[1], 1, start_index)
    share_contract = own_share(totals[2], contract_weight.shape[1], 1, start_index)
    share_fourier = own_share(totals[3], fourier_weight.shape[0], 0, start_index)
    vector_total = totals[4]
    hidden_total = totals[5]
    grad_norm = jnp.sqrt(squares)
    factor = jnp.minimum(1.0, CLIP_NORM / (grad_norm + 1e-06))
    new_square = adam_update(
        square_weight, square_first, square_second, share_square, factor, RATE_MATRIX
    )
    new_expand = adam_update(
        expand_weight, expand_first, expand_second, share_expand, factor, RATE_MATRIX
    )
    new_contract = adam_update(
        contract_weight, contract_first, contract_second, share_contract, factor, RATE_MATRIX
    )
    new_fourier = adam_update(
        fourier_weight, fourier_first, fourier_second, share_fourier, factor, RATE_MATRIX
    )
    new_vector = adam_update(
        vector_weight, vector_first, vector_second, vector_total, factor, RATE_VECTOR
    )
    new_hidden = adam_update(
        hidden_weight, hidden_first, hidden_second, hidden_total, factor, RATE_VECTOR
    )
    return (
        output.astype(jnp.bfloat16),
        grad_inputs,
        grad_norm,
        new_square[0],
        new_square[1],
        new_square[2],
        new_expand[0],
        new_expand[1],
        new_expand[2],
        new_contract[0],
        new_contract[1],
        new_contract[2],
        new_fourier[0],
        new_fourier[1],
        new_fourier[2],
        new_vector[0],
        new_vector[1],
        new_vector[2],
        new_hidden[0],
        new_hidden[1],
        new_hidden[2],
    )


GROUP = 8
TILE = 1024
PUT = 512
LANES = 128
E_BITS = E.bit_length() - 1
PIECES = 4
VMEM_BYTES = 64 * 1024 * 1024


def dot(left, right):
    return jnp.dot(left, right, preferred_element_type=jnp.float32)


def dot_bt(left, right):
    return lax.dot_general(
        left, right, (((1,), (1,)), ((), ())), preferred_element_type=jnp.float32
    )


def dot_at(left, right):
    return lax.dot_general(
        left, right, (((0,), (0,)), ((), ())), preferred_element_type=jnp.float32
    )


def low(values):
    return values.astype(jnp.bfloat16)


def column_norm(values):
    inverse = 1.0 / values.shape[0]
    centred = values - jnp.sum(values, axis=0, keepdims=True) * inverse
    variance = jnp.sum(centred * centred, axis=0, keepdims=True) * inverse
    root_inv = lax.rsqrt(variance + NORM_EPS)
    return (centred * root_inv, root_inv)


def column_norm_back(upstream, scaled, root_inv, gain):
    inverse = 1.0 / upstream.shape[0]
    through = upstream * gain
    centre = jnp.sum(through, axis=0, keepdims=True) * inverse
    along = jnp.sum(through * scaled, axis=0, keepdims=True) * inverse
    return root_inv * (through - centre - scaled * along)


def gelu_both(values):
    square = values * values
    half = 0.5 + 0.5 * jnp.tanh(values * (GELU_C + (GELU_C * GELU_A) * square))
    slope = half + values * (half * (1.0 - half)) * (
        2.0 * GELU_C + (6.0 * GELU_C * GELU_A) * square
    )
    return (values * half, slope)


def turn(values, cosine, sine, sign):
    quarter = E // 4
    first_cos, second_cos = cosine[:quarter], cosine[quarter:]
    first_sin, second_sin = sine[:quarter] * sign, sine[quarter:] * sign
    parts = []
    for base in range(0, values.shape[0], E):
        one, two, three, four = (
            values[base + quarter * step : base + quarter * (step + 1)] for step in range(4)
        )
        parts += [
            one * first_cos - two * first_sin,
            two * first_cos + one * first_sin,
            three * second_cos - four * second_sin,
            four * second_cos + three * second_sin,
        ]
    return jnp.concatenate(parts, axis=0)


def head_of(index):
    return lax.shift_right_logical(index, E_BITS)


def compress(full):
    width = full.shape[1]
    head = head_of(lax.broadcasted_iota(jnp.int32, (E, width), 1))
    result = full[:E]
    for index in range(1, H):
        result = jnp.where(head == index, full[E * index : E * (index + 1)], result)
    return result


def lane_sum(values):
    result = values[:, :LANES]
    for start in range(LANES, values.shape[1], LANES):
        result = result + values[:, start : start + LANES]
    return result


def remote(source, target, send_sem, recv_sem, device):
    return pltpu.make_async_remote_copy(
        src_ref=source,
        dst_ref=target,
        send_sem=send_sem,
        recv_sem=recv_sem,
        device_id=(device,),
        device_id_type=pl.DeviceIdType.MESH,
    )


class Place:
    def __init__(self, devices):
        self.devices = devices
        self.outers = devices // GROUP
        self.me = lax.axis_index("pts")
        self.inner = lax.rem(self.me, GROUP)
        self.outer = lax.div(self.me, GROUP)
        self.core = lax.rem(self.me, 2)
        self.pair = lax.div(self.inner, 2)
        self.chips = devices // 2
        self.chip = lax.div(self.me, 2)

    def chip_at(self, step):
        return lax.rem(self.chip + step, self.chips)

    def inner_at(self, step):
        return lax.rem(self.inner + step, GROUP)

    def outer_at(self, step):
        return lax.rem(self.outer + step, self.outers)

    def pair_at(self, step):
        return lax.rem(self.pair + step, 4)

    def device(self, outer, inner):
        return outer * GROUP + inner


class Gather:
    def __init__(self, place, buffer, scratch, slots):
        self.place, self.buffer = place, buffer
        self.send, self.recv = scratch.sem_send, scratch.sem_recv
        self.slots = slots

    def first(self, step, start):
        at = self.place
        slot = self.buffer.at[at.core, at.pair, at.outer if start else at.outer_at(step)]
        mine = self.buffer.at[at.core, at.pair, at.outer]
        source = at.outer if start else at.outer_at(step)
        return remote(
            mine, slot, self.send.at[self.slots[0], self.slots[1] + step],
            self.recv.at[self.slots[0], self.slots[1] + source],
            at.device(at.outer_at(step), at.inner),
        )

    def second(self, step, start):
        at = self.place
        source = at.pair if start else at.pair_at(step)
        return remote(
            self.buffer.at[at.core, at.pair], self.buffer.at[at.core, source],
            self.send.at[2, self.slots[2] + step], self.recv.at[2, self.slots[2] + source],
            at.device(at.outer, at.pair_at(step) * 2 + at.core),
        )

    def third(self, start):
        at = self.place
        source = at.core if start else 1 - at.core
        return remote(
            self.buffer.at[at.core], self.buffer.at[source], self.send.at[2, self.slots[3]],
            self.recv.at[2, self.slots[3]], at.device(at.outer, at.pair * 2 + 1 - at.core),
        )

    def start_first(self):
        for step in range(1, self.place.outers):
            self.first(step, True).start()

    def start_second(self):
        for step in range(1, self.place.outers):
            self.first(step, False).wait()
        for step in range(1, 4):
            self.second(step, True).start()

    def start_third(self):
        for step in range(1, 4):
            self.second(step, False).wait()
        self.third(True).start()

    def finish(self):
        self.third(False).wait()


class ChipSum:
    def __init__(self, place, scratch, key):
        self.place = place
        self.full, self.half, self.others = (
            getattr(scratch, name + key) for name in ("chip_full_", "chip_half_", "chip_others_")
        )
        self.send, self.recv = scratch.sem_send, scratch.sem_recv

    def swap(self):
        at = self.place
        return remote(
            self.full.at[1 - at.core], self.half, self.send.at[2, 0], self.recv.at[2, 0],
            at.chip * 2 + 1 - at.core,
        )

    def cross(self, step, start):
        at = self.place
        source = at.chip if start else at.chip_at(step)
        return remote(
            self.half.at[at.chip_at(step)], self.others.at[source], self.send.at[0, step],
            self.recv.at[0, source], at.chip_at(step) * 2 + at.core,
        )

    def start(self):
        self.swap().start()

    def middle(self):
        at = self.place
        self.swap().wait()
        self.half[...] = low(
            self.full[at.core].astype(jnp.float32) + self.half[...].astype(jnp.float32)
        )
        for step in range(1, at.chips):
            self.cross(step, True).start()

    def total(self):
        at = self.place
        total = self.half[at.chip].astype(jnp.float32)
        for step in range(1, at.chips):
            self.cross(step, False).wait()
            total = total + self.others[at.chip_at(step)].astype(jnp.float32)
        return total


class TableSum(ChipSum):
    def __init__(self, place, scratch):
        super().__init__(place, scratch, "t")
        self.s = scratch

    def share(self, step, start, result):
        at = self.place
        source = at.chip if start else at.chip_at(step)
        return remote(
            result.at[at.core, at.chip], result.at[at.core, source], self.send.at[1, step],
            self.recv.at[1, source], at.chip_at(step) * 2 + at.core,
        )

    def swap_back(self, start, result):
        at = self.place
        source = at.core if start else 1 - at.core
        return remote(
            result.at[at.core], result.at[source], self.send.at[2, 1], self.recv.at[2, 1],
            at.chip * 2 + 1 - at.core,
        )

    def start(self):
        s = self.s
        table = low(dot(s.spread[...], s.per_block[...]))
        for chunk in range(self.place.devices):
            self.full[chunk % 2, chunk // 2] = table[chunk * 16 : (chunk + 1) * 16]
        super().start()

    def late(self, result):
        at, s = self.place, self.s
        result[at.core, at.chip] = low(self.total() * s.inverse[0:1, :])
        for step in range(1, at.chips):
            self.share(step, True, result).start()

    def last(self, result):
        for step in range(1, self.place.chips):
            self.share(step, False, result).wait()
        self.swap_back(True, result).start()

    def finish(self, result):
        self.swap_back(False, result).wait()


class GradSum:
    def __init__(self, place, scratch, key, first):
        self.place = place
        self.half, self.quarter, self.last = (
            getattr(scratch, name + key) for name in ("half_", "quarter_", "last_")
        )
        self.full = scratch.gather_two.at[:, :, :, first : first + self.last.shape[1]]
        self.send, self.recv = scratch.sem_send, scratch.sem_recv

    def swap(self):
        at = self.place
        return remote(
            self.full.at[1 - at.core], self.half, self.send.at[2, 7], self.recv.at[2, 7],
            at.device(at.outer, at.pair * 2 + 1 - at.core),
        )

    def across(self, step, start):
        at = self.place
        source = at.pair if start else at.pair_at(step)
        return remote(
            self.half.at[at.pair_at(step)], self.quarter.at[source], self.send.at[2, 8 + step],
            self.recv.at[2, 8 + source], at.device(at.outer, at.pair_at(step) * 2 + at.core),
        )

    def along(self, step, start):
        at = self.place
        source = at.outer if start else at.outer_at(step)
        return remote(
            self.quarter.at[at.pair, at.outer_at(step)], self.last.at[source], self.send.at[2, 12 + step],
            self.recv.at[2, 12 + source], at.device(at.outer_at(step), at.inner),
        )

    def start(self, chunk_of):
        at = self.place

        @pl.loop(0, at.devices)
        def _(chunk):
            inner = lax.rem(chunk, GROUP)
            self.full[lax.rem(inner, 2), lax.div(inner, 2), lax.div(chunk, GROUP)] = low(
                chunk_of(chunk)
            )

        self.swap().start()

    def second(self):
        at = self.place
        self.swap().wait()

        @pl.loop(0, 4)
        def _(pair):
            self.half[pair] = low(
                self.full[at.core, pair].astype(jnp.float32) + self.half[pair].astype(jnp.float32)
            )

        for step in range(1, 4):
            self.across(step, True).start()

    def third(self):
        at = self.place
        total = self.half[at.pair].astype(jnp.float32)
        for step in range(1, 4):
            self.across(step, False).wait()
            total = total + self.quarter[at.pair_at(step)].astype(jnp.float32)
        self.quarter[at.pair] = low(total)
        for step in range(1, at.outers):
            self.along(step, True).start()

    def finish(self):
        at = self.place
        total = self.quarter[at.pair, at.outer].astype(jnp.float32)
        for step in range(1, at.outers):
            self.along(step, False).wait()
            total = total + self.last[at.outer_at(step)].astype(jnp.float32)
        return total


def layer_kernel(names, devices, *refs):
    s = types.SimpleNamespace(**dict(zip(names, refs)))
    at = Place(devices)
    points, width = s.features_far.shape
    tiles = points // TILE
    blocks = points // BLOCK
    share = width // devices
    tile_blocks = TILE // BLOCK
    f32 = jnp.float32

    barrier = pltpu.get_barrier_semaphore()
    pl.semaphore_signal(
        barrier, inc=1, device_id=(at.chip * 2 + 1 - at.core,),
        device_id_type=pl.DeviceIdType.MESH,
    )
    for step in range(1, at.chips):
        pl.semaphore_signal(
            barrier, inc=1, device_id=(at.chip_at(step) * 2 + at.core,),
            device_id_type=pl.DeviceIdType.MESH,
        )

    def tile_load(source, tile):
        slot = lax.rem(tile, 2)
        where = pl.ds(pl.multiple_of(tile * TILE, TILE), TILE)
        return pltpu.make_async_copy(
            source.at[where, :], s.load_slots.at[slot], s.sem_in.at[slot]
        )

    for tile in range(2):
        tile_load(s.features_far, tile).start()

    class Aside:
        def __init__(self, first, *buffers):
            self.pairs = []
            row = first
            for buffer in buffers:
                for start in range(0, buffer.shape[0], width):
                    near = buffer.at[start : start + width]
                    far = s.aside.at[row : row + width]
                    self.pairs.append((near, far, s.sem_aside.at[row // width]))
                    row += width

        def store(self):
            for near, far, sem in self.pairs:
                pltpu.make_async_copy(near, far, sem).start()

        def stored(self):
            for near, far, sem in self.pairs:
                pltpu.make_async_copy(near, far, sem).wait()

        def load(self):
            for near, far, sem in self.pairs:
                pltpu.make_async_copy(far, near, sem).start()

        def loaded(self):
            for near, far, sem in self.pairs:
                pltpu.make_async_copy(far, near, sem).wait()

    aside_a = Aside(0, s.u1, s.kv)
    aside_b = Aside(3 * width, s.e1, s.o, s.u2, s.u3)

    def columns(tile):
        return pl.ds(pl.multiple_of(tile * TILE, TILE), TILE)

    def block_columns(block):
        return pl.ds(pl.multiple_of(block * BLOCK, BLOCK), BLOCK)

    def column(index):
        return s.cols[:, index : index + 1]

    def hidden_column(index):
        return jnp.concatenate([column(8 + 2 * index), column(9 + 2 * index)], axis=0)

    def out_copy(tile, source, target):
        where = pl.ds(pl.multiple_of(tile * TILE, TILE), TILE)
        return pltpu.make_async_copy(
            source.at[:, where], target.at[:, where], s.sem_out.at[tile]
        )

    def end_out(source, target):
        for tile in range(tiles):
            out_copy(tile, source, target).wait()

    def pack_square(matrix):
        for row in range(share):
            s.pack[matrix * share + row : matrix * share + row + 1, :] = s.square_weight[
                matrix : matrix + 1, row * width : (row + 1) * width
            ]

    split = s.gather_one.shape[3]
    for matrix in range(4):
        pack_square(matrix)
    s.gather_one[at.core, at.pair, at.outer] = low(s.pack[:split, :])
    pl.semaphore_wait(barrier, at.chips)
    one = Gather(at, s.gather_one, s, (1, 0, 2, 6))
    two = Gather(at, s.gather_two, s, (2, 12, 8, 7))
    one.start_first()

    for matrix in range(4, 7):
        pack_square(matrix)
    for matrix in range(2):
        for half in range(2):
            for row in range(share):
                place = (7 + 2 * matrix + half) * share + row
                start = row * F + half * width
                s.pack[place : place + 1, :] = s.expand_weight[
                    matrix : matrix + 1, start : start + width
                ]
        for row in range(2 * share):
            place = (11 + 2 * matrix) * share + row
            s.pack[place : place + 1, :] = s.contract_weight[
                matrix : matrix + 1, row * width : (row + 1) * width
            ]
    s.pack[15 * share : 16 * share, :LANES] = s.fourier_weight[...]
    s.pack[15 * share : 16 * share, LANES:] = jnp.zeros((share, LANES), f32)
    live = s.point_mask[...].astype(f32)
    counts = dot_bt(jnp.ones((8, LANES), jnp.bfloat16), low(live))
    s.pack[15 * share : 15 * share + 1, LANES : LANES + blocks] = counts[:1]
    lane = lax.broadcasted_iota(jnp.int32, (1, LANES), 1)
    wide_block = head_of(lax.broadcasted_iota(jnp.int32, (1, E * blocks), 1))
    item_row = jnp.zeros((1, LANES), f32)
    item_wide = jnp.zeros((1, E * blocks), jnp.int32)
    for block in range(blocks):
        item_row = jnp.where(lane == block, s.items[block].astype(f32), item_row)
        item_wide = jnp.where(wide_block == block, s.items[block], item_wide)
    s.pack[15 * share + 1 : 15 * share + 2, LANES:] = item_row
    s.gather_two[at.core, at.pair, at.outer] = low(s.pack[split:, :])

    row_at = lax.broadcasted_iota(jnp.int32, (width, width), 0)
    lane_at = lax.broadcasted_iota(jnp.int32, (width, width), 1)
    s.eye[...] = jnp.where(row_at == lane_at, 1.0, 0.0).astype(jnp.bfloat16)
    s.heads[...] = jnp.where(head_of(row_at) == head_of(lane_at), 1.0, 0.0).astype(jnp.bfloat16)
    s.small[...] = jnp.zeros(s.small.shape, f32)
    s.small[0:8, :] = s.vector_weight[...]
    for row in range(2):
        for half in range(2):
            s.small[8 + 2 * row + half : 9 + 2 * row + half, :] = s.hidden_weight[
                row : row + 1, half * width : (half + 1) * width
            ]
    s.small[12:14, : FOUR // 2] = s.fourier_basis[...]
    s.cols[...] = s.small[...].T
    rows_wide = lax.broadcasted_iota(jnp.int32, s.spread.shape, 0)
    lanes_wide = lax.broadcasted_iota(jnp.int32, s.spread.shape, 1)
    s.spread[...] = jnp.where(
        (item_wide == head_of(rows_wide)) & (((rows_wide ^ lanes_wide) & (E - 1)) == 0), 1.0, 0.0
    ).astype(jnp.bfloat16)
    s.vector_sum[...] = jnp.zeros(s.vector_sum.shape, f32)
    speed = (lax.broadcasted_iota(jnp.int32, (E // 4, 1), 0).astype(f32) + 1.0) * (
        math.pi / (E // 4)
    )

    def add_sum(index, values):
        for part in range(values.shape[0] // width):
            s.vector_sum[index + part] += lane_sum(values[part * width : (part + 1) * width])

    def turned_load(source, tile):
        tile_load(source, tile).wait()
        turned = dot_bt(s.eye[...], s.load_slots[lax.rem(tile, 2)])

        @pl.when(tile + 2 < tiles)
        def _():
            tile_load(source, tile + 2).start()

        return turned

    def norm_one(tile, _):
        where = columns(tile)
        turned = turned_load(s.features_far, tile)
        s.turned[:, where] = low(turned)
        scaled, root = column_norm(turned)
        s.root_one[0:1, where] = root
        s.u1[:, where] = low(scaled * column(0) + column(1))

    def fourier_part(tile, _):
        where = pl.ds(pl.multiple_of(tile * PUT, PUT), PUT)
        x_row, y_row = s.coords[0:1, where], s.coords[1:2, where]
        basis = s.cols[: FOUR // 2, :]
        phases = 2.0 * math.pi * (basis[:, 12:13] * x_row + basis[:, 13:14] * y_row)
        s.phi[:, where] = low(jnp.concatenate([jnp.cos(phases), jnp.sin(phases)], axis=0))

    def angle_part(tile, _):
        where = pl.ds(pl.multiple_of(tile * PUT, PUT), PUT)
        angles = jnp.concatenate(
            [speed * s.coords[0:1, where], speed * s.coords[1:2, where]], axis=0
        )
        s.cosine[:, where] = jnp.cos(angles)
        s.sine[:, where] = jnp.sin(angles)
        for block in range(PUT // BLOCK):
            s.mask[0:1, pl.ds(pl.multiple_of(tile * PUT + block * BLOCK, BLOCK), BLOCK)] = (
                s.point_mask[pl.ds(tile * (PUT // BLOCK) + block, 1), :].astype(f32)
            )

    parts = points // PUT
    lax.fori_loop(0, tiles, norm_one, None)
    one.start_second()
    two.start_first()
    lax.fori_loop(0, 3 * parts // 4, fourier_part, None)
    one.start_third()
    two.start_second()
    lax.fori_loop(0, parts, angle_part, None)
    one.finish()

    group = 16 // share

    def chunk_pair(buffer, index):
        parts = []
        for step in range(group):
            chunk = index * group + step
            inner = lax.rem(chunk, GROUP)
            parts.append(
                buffer[lax.rem(inner, 2), lax.div(inner, 2), lax.div(chunk, GROUP)].astype(f32)
            )
        return parts

    def join(parts, piece):
        return low(
            jnp.concatenate([part[piece * share : (piece + 1) * share] for part in parts], axis=0)
        )

    @pl.loop(0, devices // group)
    def _(index):
        parts = chunk_pair(s.gather_one, index)
        where = pl.ds(pl.multiple_of(index * 16, 16), 16)
        for piece in range(3):
            s.w_qkv[where, piece * width : (piece + 1) * width] = join(parts, piece)
        s.w_o[where, :] = join(parts, 3)

    def flip(matrix):
        return low(dot_bt(s.eye[...], matrix))

    for piece in range(3):
        s.t_qkv[piece * width : (piece + 1) * width, :] = flip(
            s.w_qkv[:, piece * width : (piece + 1) * width]
        )
    s.t_o[...] = flip(s.w_o[...])

    def block_product(left, right):
        return compress(dot_bt(left, right))

    def put_products(tile, left, right):
        for block in range(tile_blocks):
            lanes = slice(block * BLOCK, (block + 1) * BLOCK)
            where = pl.ds(pl.multiple_of((tile * tile_blocks + block) * E, E), E)
            s.per_block[where, :] = low(block_product(left[:, lanes], right[:, lanes]))

    def summary(table, tile, block):
        item = s.items[tile * tile_blocks + block]
        rows = jnp.concatenate([table[0, item], table[1, item]], axis=0)
        return jnp.concatenate([rows] * H, axis=0) * s.heads[...]

    def per_block(tile, function):
        return jnp.concatenate([function(block) for block in range(tile_blocks)], axis=1)

    def lanes_of(block):
        return slice(block * BLOCK, (block + 1) * BLOCK)

    def phase_a(tile, _):
        where = columns(tile)
        projected = dot(s.t_qkv[...], s.u1[:, where])
        cosine, sine = s.cosine[:, where], s.sine[:, where]
        s.q[:, where] = low(turn(projected[:width], cosine, sine, 1.0))
        keys = low(turn(projected[width : 2 * width], cosine, sine, 1.0) * s.mask[0:1, where])
        values = low(projected[2 * width :])
        s.kv[:width, where] = keys
        s.kv[width:, where] = values
        put_products(tile, values, keys)

    lax.fori_loop(0, tiles, phase_a, None)
    table_sum = TableSum(at, s)
    table_sum.start()
    aside_a.store()
    table_sum.middle()
    lax.fori_loop(3 * parts // 4, parts, fourier_part, None)
    two.start_third()

    def take_two(index, carried):
        parts = chunk_pair(s.gather_two, index)
        where = pl.ds(pl.multiple_of(index * 16, 16), 16)
        for piece in range(2):
            s.w_kv[where, piece * width : (piece + 1) * width] = join(parts, piece)
            s.w_w1[where, piece * width : (piece + 1) * width] = join(parts, 3 + piece)
            s.w_p1[where, piece * width : (piece + 1) * width] = join(parts, 5 + piece)
        s.w_do[where, :] = join(parts, 2)
        both = pl.ds(pl.multiple_of(index * 32, 32), 32)
        for piece, target in ((7, s.w_w2), (9, s.w_p2)):
            target[both, :] = low(
                jnp.concatenate([part[piece * share : (piece + 2) * share] for part in parts], axis=0)
            )
        for part in parts:
            count_row = part[11 * share : 11 * share + 1, LANES:]
            item_at = part[11 * share + 1 : 11 * share + 2, LANES:]
            carried = carried + jnp.where(item_at == own_item, count_row, 0.0)
        s.fourier[where, :] = jnp.concatenate(
            [part[11 * share : 12 * share, :LANES] for part in parts], axis=0
        )
        return carried

    two.finish()
    own_item = at.chip.astype(f32)
    found = lax.fori_loop(0, devices // group, take_two, jnp.zeros((1, LANES), f32))
    s.inverse[0:1, :] = jnp.broadcast_to(1.0 / jnp.sum(found, axis=1, keepdims=True), (1, width))
    w_dq = jnp.concatenate(
        [s.fourier[pl.ds(0, FOUR, stride=2), :], s.fourier[pl.ds(1, FOUR, stride=2), :]], axis=1
    )
    s.t_dq[...] = low(w_dq.T)
    table_sum.late(s.table_self)
    for piece in range(2):
        cols = slice(piece * width, (piece + 1) * width)
        s.t_kv[cols, :] = flip(s.w_kv[:, cols])
        s.t_w1[cols, :] = flip(s.w_w1[:, cols])
        s.t_p1[cols, :] = flip(s.w_p1[:, cols])
        s.t_w2[:, cols] = flip(s.w_w2[cols, :])
        s.t_p2[:, cols] = flip(s.w_p2[cols, :])
    s.t_do[...] = flip(s.w_do[...])
    table_sum.last(s.table_self)
    table_sum.finish(s.table_self)

    def phase_b(tile, _):
        where = columns(tile)
        mask = s.mask[0:1, where]
        queries = s.q[:, where]
        mixed = per_block(
            tile, lambda b: dot(summary(s.table_self, tile, b), queries[:, lanes_of(b)])
        )
        attended = low(mixed * mask)
        s.o[:, where] = attended
        first_sum = s.turned[:, where].astype(f32) + dot(s.t_o[...], attended)
        scaled_two, root_two = column_norm(first_sum)
        s.root_two[0:1, where] = root_two
        s.xh2[:, where] = low(scaled_two)
        middle = low(scaled_two * column(2) + column(3))
        s.u2[:, where] = middle
        hidden_pre = dot(s.t_w1[...], middle) + hidden_column(0)
        hidden = low(gelu(hidden_pre))
        s.e1[:, where] = hidden
        s.slope[:, where] = low(hidden_pre)
        encoded = first_sum + dot(s.t_w2[...], hidden) + column(6)
        scaled_three, root_three = column_norm(encoded)
        s.root_three[0:1, where] = root_three
        s.xh3[:, where] = low(scaled_three)
        outer = low(scaled_three * column(4) + column(5))
        s.u3[:, where] = outer
        pair = dot(s.t_kv[...], outer)
        keys = low(pair[:width] * mask)
        values = low(pair[width:])
        s.kvd[:width, where] = keys
        s.kvd[width:, where] = values
        put_products(tile, values, keys)

    lax.fori_loop(0, tiles, phase_b, None)
    table_sum.start()
    aside_b.store()
    table_sum.middle()

    for tile in range(2):
        tile_load(s.cotangent_far, tile).start()
    aside_a.stored()

    def cross_inputs(tile, _):
        where = columns(tile)
        s.qd[:, where] = low(dot(s.t_dq[...], s.phi[:, where]))
        turned = turned_load(s.cotangent_far, tile)
        add_sum(7, turned)
        turned = low(turned)
        s.u1[:, where] = turned
        s.kv[:, where] = low(dot(s.w_p2[...], turned))

    def slopes(tile, _):
        where = columns(tile)
        s.slope[:, where] = low(gelu_slope(s.slope[:, where].astype(f32)))

    lax.fori_loop(0, tiles, cross_inputs, None)
    table_sum.late(s.table_other)
    lax.fori_loop(0, tiles, slopes, None)
    aside_b.stored()
    table_sum.last(s.table_other)
    table_sum.finish(s.table_other)

    def phase_c(tile, _):
        where = columns(tile)
        mask = s.mask[0:1, where]
        queries = s.qd[:, where]
        tables = [summary(s.table_other, tile, block) for block in range(tile_blocks)]
        decoded = low(
            per_block(tile, lambda b: dot(tables[b], queries[:, lanes_of(b)])) * mask
        )
        s.u2[:, where] = decoded
        latent_low = low(dot(s.t_do[...], decoded))
        s.o[:, where] = latent_low
        hidden, slope = gelu_both(dot(s.t_p1[...], latent_low) + hidden_column(1))
        s.e1[:, where] = low(hidden)
        grad_spread = s.kv[:, where].astype(f32) * slope
        add_sum(10, grad_spread)
        grad_spread = low(grad_spread)
        s.kv[:, where] = grad_spread
        grad_latent = low(s.u1[:, where].astype(f32) + dot(s.w_p1[...], grad_spread))
        s.u3[:, where] = grad_latent
        grad_decoded = low(dot(s.w_do[...], grad_latent) * mask)
        put_products(tile, grad_decoded, queries)
        s.qd[:, where] = grad_decoded

    lax.fori_loop(0, tiles, phase_c, None)
    table_sum.start()
    table_sum.middle()

    def cross_query_grads(tile, _):
        where = columns(tile)
        upstream = s.qd[:, where]
        grad = per_block(
            tile, lambda b: dot_at(summary(s.table_other, tile, b), upstream[:, lanes_of(b)])
        )
        s.qd[:, where] = low(grad)

    def outputs(tile, _):
        where = columns(tile)
        output = dot(s.t_do[...], s.u2[:, where]) + dot(s.t_p2[...], s.e1[:, where]) + column(7)
        s.qd[:, where] = low(output)
        out_copy(tile, s.qd, s.layer_output).start()

    lax.fori_loop(0, tiles, cross_query_grads, None)
    s.grad_dq[...] = dot_bt(s.phi[...], s.qd[...])
    s.fourier[pl.ds(0, FOUR, stride=2), :] = s.grad_dq[:, :LANES]
    s.fourier[pl.ds(1, FOUR, stride=2), :] = s.grad_dq[:, LANES:]
    s.grad_do[...] = dot_bt(s.u2[...], s.u3[...])
    table_sum.late(s.table_third)
    s.grad_p1[...] = dot_bt(s.o[...], s.kv[...])
    s.grad_p2[...] = dot_bt(s.e1[...], s.u1[...])
    zeros = jnp.zeros((share, LANES), f32)

    def rows_of(chunk, count=1):
        size = share * count
        return pl.ds(pl.multiple_of(chunk * size, size), size)

    def chunk_c(chunk):
        where = rows_of(chunk)
        return jnp.concatenate(
            [
                s.grad_do[where, :],
                s.grad_p1[where, :width],
                s.grad_p1[where, width:],
                s.grad_p2[rows_of(chunk, 2), :],
                jnp.concatenate([s.fourier[where, :], zeros], axis=1),
            ],
            axis=0,
        )

    sum_c = GradSum(at, s, "c", 0)
    sum_c.start(chunk_c)
    lax.fori_loop(0, tiles, outputs, None)
    table_sum.last(s.table_third)
    end_out(s.qd, s.layer_output)
    aside_a.load()
    aside_b.load()
    sum_c.second()
    table_sum.finish(s.table_third)

    def phase_d(tile, _):
        where = columns(tile)
        mask = s.mask[0:1, where]
        keys, values = s.kvd[:width, where], s.kvd[width:, where]
        tables = [summary(s.table_third, tile, block) for block in range(tile_blocks)]
        grad_keys = per_block(tile, lambda b: dot_at(tables[b], values[:, lanes_of(b)])) * mask
        grad_values = per_block(tile, lambda b: dot(tables[b], keys[:, lanes_of(b)]))
        grad_pair = low(jnp.concatenate([grad_keys, grad_values], axis=0))
        s.kvd[:, where] = grad_pair
        grad_outer = dot(s.w_kv[...], grad_pair)
        scaled = s.xh3[:, where].astype(f32)
        add_sum(4, grad_outer * scaled)
        add_sum(5, grad_outer)
        grad_encoded = column_norm_back(
            grad_outer, scaled, s.root_three[0:1, where], column(4)
        )
        add_sum(6, grad_encoded)
        grad_encoded_low = low(grad_encoded)
        s.xh3[:, where] = grad_encoded_low
        grad_hidden = dot(s.w_w2[...], grad_encoded_low) * s.slope[:, where].astype(f32)
        add_sum(8, grad_hidden)
        grad_hidden = low(grad_hidden)
        s.slope[:, where] = grad_hidden
        grad_middle = dot(s.w_w1[...], grad_hidden)
        scaled = s.xh2[:, where].astype(f32)
        add_sum(2, grad_middle * scaled)
        add_sum(3, grad_middle)
        grad_first = grad_encoded + column_norm_back(
            grad_middle, scaled, s.root_two[0:1, where], column(2)
        )
        grad_first = low(grad_first)
        s.xh2[:, where] = grad_first
        grad_attended = low(dot(s.w_o[...], grad_first) * mask)
        s.qd[:, where] = grad_attended
        put_products(tile, grad_attended, s.q[:, where])

    lax.fori_loop(0, tiles // 2, phase_d, None)
    sum_c.third()
    lax.fori_loop(tiles // 2, tiles, phase_d, None)
    table_sum.start()
    s.grads_c[...] = sum_c.finish()
    table_sum.middle()
    aside_a.loaded()
    aside_b.loaded()

    def query_grads(tile, _):
        where = columns(tile)
        upstream = s.qd[:, where]
        grad = per_block(
            tile, lambda b: dot_at(summary(s.table_self, tile, b), upstream[:, lanes_of(b)])
        )
        s.q[:, where] = low(turn(grad, s.cosine[:, where], s.sine[:, where], -1.0))

    lax.fori_loop(0, tiles, query_grads, None)
    s.grad_o[...] = dot_bt(s.o[...], s.xh2[...])
    s.grad_qkv[:, :width] = dot_bt(s.u1[...], s.q[...])
    table_sum.late(s.table_other)
    s.grad_kv[...] = dot_bt(s.u3[...], s.kvd[...])
    s.grad_w2[...] = dot_bt(s.e1[...], s.xh3[...])
    s.grad_w1[...] = dot_bt(s.u2[...], s.slope[...])

    def chunk_d(chunk):
        where = rows_of(chunk)
        return jnp.concatenate(
            [
                s.grad_kv[where, :width],
                s.grad_kv[where, width:],
                s.grad_o[where, :],
                s.grad_w1[where, :width],
                s.grad_w1[where, width:],
                s.grad_w2[rows_of(chunk, 2), :],
                s.grad_qkv[where, :width],
            ],
            axis=0,
        )

    sum_d = GradSum(at, s, "d", 0)
    sum_d.start(chunk_d)
    table_sum.last(s.table_other)
    table_sum.finish(s.table_other)
    sum_d.second()

    def phase_e(tile, _):
        where = columns(tile)
        mask = s.mask[0:1, where]
        keys, values = s.kv[:width, where], s.kv[width:, where]
        tables = [summary(s.table_other, tile, block) for block in range(tile_blocks)]
        grad_keys = per_block(tile, lambda b: dot_at(tables[b], values[:, lanes_of(b)])) * mask
        grad_values = low(per_block(tile, lambda b: dot(tables[b], keys[:, lanes_of(b)])))
        s.kv[:width, where] = low(turn(grad_keys, s.cosine[:, where], s.sine[:, where], -1.0))
        s.kv[width:, where] = grad_values

    lax.fori_loop(0, tiles, phase_e, None)
    s.grad_qkv[:, width:] = dot_bt(s.u1[...], s.kv[...])
    sum_e = ChipSum(at, s, "e")

    @pl.loop(0, devices)
    def _(chunk):
        where = rows_of(chunk)
        s.chip_full_e[lax.rem(chunk, 2), lax.div(chunk, 2)] = low(
            jnp.concatenate(
                [s.grad_qkv[where, width : 2 * width], s.grad_qkv[where, 2 * width :]], axis=0
            )
        )

    sum_e.start()

    def phase_f(tile, _):
        where = columns(tile)
        grad_normed = dot(
            s.w_qkv[...], jnp.concatenate([s.q[:, where], s.kv[:, where]], axis=0)
        )
        turned = s.turned[:, where].astype(f32)
        root = s.root_one[0:1, where]
        scaled = (turned - jnp.sum(turned, axis=0, keepdims=True) * (1.0 / width)) * root
        add_sum(0, grad_normed * scaled)
        add_sum(1, grad_normed)
        grad_input = s.xh2[:, where].astype(f32) + column_norm_back(
            grad_normed, scaled, root, column(0)
        )
        s.xh2[:, where] = low(grad_input)
        out_copy(tile, s.xh2, s.input_grad).start()

    sum_d.third()
    sum_e.middle()
    lax.fori_loop(0, tiles, phase_f, None)
    end_out(s.xh2, s.input_grad)
    s.grads_d[...] = sum_d.finish()
    s.grads_e[...] = sum_e.total()
    squares = sum(
        jnp.sum(grads[...] * grads[...], axis=0, keepdims=True)
        for grads in (s.grads_c, s.grads_d, s.grads_e)
    )

    lane_wide = lax.broadcasted_iota(jnp.int32, (width, LANES), 1)
    sums = jnp.zeros((width, LANES), f32)
    for index in range(12):
        sums = jnp.where(
            lane_wide == index, jnp.sum(s.vector_sum[index], axis=1, keepdims=True), sums
        )
    s.vector_cols[...] = sums
    turned_sums = s.vector_cols[...].T
    high = low(squares).astype(f32)
    s.final_near[at.core] = low(
        jnp.concatenate(
            [turned_sums[:12], high, squares - high, jnp.zeros((2, width), f32)], axis=0
        )
    )

    def final_core(start):
        source = at.core if start else 1 - at.core
        return remote(
            s.final_near.at[at.core], s.final_near.at[source], s.sem_send.at[2, 1],
            s.sem_recv.at[2, 1], at.chip * 2 + 1 - at.core,
        )

    def final_chips(step, start):
        source = at.chip if start else at.chip_at(step)
        return remote(
            s.final_far.at[at.chip], s.final_far.at[source], s.sem_send.at[1, step],
            s.sem_recv.at[1, source], at.chip_at(step) * 2 + at.core,
        )

    final_core(True).start()
    final_core(False).wait()
    total = s.final_near[0].astype(f32) + s.final_near[1].astype(f32)
    square_sum = total[12:13] + total[13:14]
    high = low(square_sum).astype(f32)
    s.final_far[at.chip] = low(
        jnp.concatenate([total[:12], high, square_sum - high, total[14:]], axis=0)
    )
    for step in range(1, at.chips):
        final_chips(step, True).start()
    for step in range(1, at.chips):
        final_chips(step, False).wait()
    total = s.final_far[0].astype(f32)
    for index in range(1, at.chips):
        total = total + s.final_far[index].astype(f32)
    s.vector_all[...] = total


def update_kernel(share, *refs):
    sources, refs = refs[:2], refs[2:]
    grads_c, grads_d, grads_e, vector_all = refs[:4]
    weights_far = refs[4:22]
    targets = refs[22:24]
    norm_out = refs[24]
    results = refs[25:43]
    flat_square, flat_expand, flat_contract, *held, sems, weight_sems = refs[43:]
    held, turned_out, weights = held[:2], held[2:4], held[4:]
    weight_loads = [
        pltpu.make_async_copy(far, near, weight_sems.at[index])
        for index, (far, near) in enumerate(zip(weights_far, weights))
    ]
    loads, stores = [], []
    size = targets[0].shape[0] // PIECES
    for piece in range(PIECES):
        where = slice(piece * size, (piece + 1) * size)
        for index in range(2):
            near = held[index].at[:, where]
            own = turned_out[index].at[where]
            loads.append(
                pltpu.make_async_copy(
                    sources[index].at[:, where], near, sems.at[0, index, piece]
                )
            )
            stores.append(
                pltpu.make_async_copy(own, targets[index].at[where], sems.at[1, index, piece])
            )
    for load in loads + weight_loads:
        load.start()
    for piece in range(PIECES):
        where = slice(piece * size, (piece + 1) * size)
        for index in range(2):
            loads[2 * piece + index].wait()
            part = held[index][:, where].astype(turned_out[index].dtype)
            turned_out[index][where] = part.T
            stores[2 * piece + index].start()
    width = grads_c.shape[1]
    places = [(grads_d, 7), (grads_e, 0), (grads_e, 1), (grads_d, 2), (grads_d, 0), (grads_d, 1), (grads_c, 0)]
    for matrix, (source, piece) in enumerate(places):
        for row in range(share):
            start = piece * share + row
            flat_square[matrix : matrix + 1, row * width : (row + 1) * width] = source[
                start : start + 1, :
            ]
    for matrix, (source, piece) in enumerate(((grads_d, 3), (grads_c, 1))):
        for half in range(2):
            for row in range(share):
                start = (piece + half) * share + row
                target = row * F + half * width
                flat_expand[matrix : matrix + 1, target : target + width] = source[
                    start : start + 1, :
                ]
    for matrix, (source, piece) in enumerate(((grads_d, 5), (grads_c, 3))):
        for row in range(2 * share):
            start = piece * share + row
            flat_contract[matrix : matrix + 1, row * width : (row + 1) * width] = source[
                start : start + 1, :
            ]
    fourier = grads_c[5 * share : 6 * share, :LANES]
    turned = vector_all[...]
    rows = jnp.sum(turned[:12] * turned[:12], axis=0, keepdims=True) + turned[12:13] + turned[13:14]
    norm = jnp.sqrt(jnp.sum(rows, axis=1, keepdims=True))
    norm_out[...] = norm
    factor = jnp.minimum(1.0, CLIP_NORM / (norm + 1e-06))
    hidden = jnp.concatenate(
        [
            jnp.concatenate([turned[8:9], turned[9:10]], axis=1),
            jnp.concatenate([turned[10:11], turned[11:12]], axis=1),
        ],
        axis=0,
    )
    for load in weight_loads:
        load.wait()
    grads = (flat_square[...], flat_expand[...], flat_contract[...], fourier, turned[:8], hidden)
    rates = (RATE_MATRIX,) * 4 + (RATE_VECTOR,) * 2
    for index, (grad, rate) in enumerate(zip(grads, rates)):
        weight, first, second = (weights[3 * index + part][...] for part in range(3))
        values = adam_update(weight, first, second, grad, factor, rate)
        for part in range(3):
            results[3 * index + part][...] = values[part]
    for store in stores:
        store.wait()


def fused(devices, features, coords, fourier_basis, block_items, point_mask, cotangent, *weights):
    points, width = features.shape
    blocks = points // BLOCK
    outers = devices // GROUP
    share = width // devices
    items = points * devices // ITEM_PTS
    bf16, f32 = jnp.bfloat16, jnp.float32
    square, expand, contract, fourier, vector, hidden = (weights[3 * i] for i in range(6))
    vmem = lambda shape, dtype: pltpu.VMEM(shape, dtype)
    inputs = {
        "items": block_items,
        "features_far": features,
        "coords": coords,
        "fourier_basis": fourier_basis,
        "point_mask": point_mask.reshape(blocks, BLOCK),
        "cotangent_far": cotangent,
        "square_weight": square,
        "expand_weight": expand,
        "contract_weight": contract,
        "fourier_weight": fourier.reshape(share, LANES),
        "vector_weight": vector,
        "hidden_weight": hidden,
    }
    rows_c, rows_d, rows_e = 6 * share, 8 * share, 2 * share
    chips = devices // 2
    outputs = {
        "layer_output": ((width, points), bf16),
        "input_grad": ((width, points), bf16),
        "grads_c": ((rows_c, width), f32),
        "grads_d": ((rows_d, width), f32),
        "grads_e": ((rows_e, width), f32),
        "vector_all": ((16, width), f32),
        "aside": ((8 * width, points), bf16),
    }
    tall = lambda rows: vmem((rows, points), bf16)
    scratch = {
        "pack": vmem((16 * share, width), f32),
        "gather_one": vmem((2, 4, outers, 4 * share, width), bf16),
        "gather_two": vmem((2, 4, outers, 12 * share, width), bf16),
        "eye": vmem((width, width), bf16),
        "heads": vmem((width, width), bf16),
        "small": vmem((LANES, width), f32),
        "cols": vmem((width, LANES), f32),
        "spread": vmem((items * E, blocks * E), bf16),
        "vector_sum": vmem((12, width, LANES), f32),
        "vector_cols": vmem((width, LANES), f32),
        "grad_qkv": vmem((width, 3 * width), f32),
        "grad_o": vmem((width, width), f32),
        "grad_kv": vmem((width, 2 * width), f32),
        "grad_do": vmem((width, width), f32),
        "grad_w1": vmem((width, F), f32),
        "grad_p1": vmem((width, F), f32),
        "grad_w2": vmem((F, width), f32),
        "grad_p2": vmem((F, width), f32),
        "grad_dq": vmem((FOUR, width), f32),
        "fourier": vmem((2 * FOUR, LANES), f32),
        "w_qkv": vmem((width, 3 * width), bf16),
        "t_qkv": vmem((3 * width, width), bf16),
        "w_o": vmem((width, width), bf16),
        "t_o": vmem((width, width), bf16),
        "w_kv": vmem((width, 2 * width), bf16),
        "t_kv": vmem((2 * width, width), bf16),
        "w_do": vmem((width, width), bf16),
        "t_do": vmem((width, width), bf16),
        "w_w1": vmem((width, F), bf16),
        "t_w1": vmem((F, width), bf16),
        "w_p1": vmem((width, F), bf16),
        "t_p1": vmem((F, width), bf16),
        "w_w2": vmem((F, width), bf16),
        "t_w2": vmem((width, F), bf16),
        "w_p2": vmem((F, width), bf16),
        "t_p2": vmem((width, F), bf16),
        "t_dq": vmem((width, FOUR), bf16),
        "mask": vmem((1, points), f32),
        "root_one": vmem((1, points), f32),
        "root_two": vmem((1, points), f32),
        "root_three": vmem((1, points), f32),
        "cosine": vmem((E // 2, points), f32),
        "sine": vmem((E // 2, points), f32),
        "phi": tall(FOUR),
        "u1": tall(width),
        "q": tall(width),
        "kv": tall(2 * width),
        "qd": tall(width),
        "o": tall(width),
        "xh2": tall(width),
        "u2": tall(width),
        "e1": tall(F),
        "slope": tall(F),
        "xh3": tall(width),
        "u3": tall(width),
        "kvd": tall(2 * width),
        "per_block": vmem((blocks * E, width), bf16),
        "inverse": vmem((8, width), f32),
        "table_self": vmem((2, chips, 16, width), bf16),
        "table_other": vmem((2, chips, 16, width), bf16),
        "final_near": vmem((2, 16, width), bf16),
        "final_far": vmem((chips, 16, width), bf16),
        "turned": tall(width),
        "sem_in": pltpu.SemaphoreType.DMA((2,)),
        "sem_aside": pltpu.SemaphoreType.DMA((8,)),
        "table_third": vmem((2, chips, 16, width), bf16),
        "load_slots": vmem((2, TILE, width), bf16),
        "sem_out": pltpu.SemaphoreType.DMA((points // TILE,)),
    }
    for key in ("t", "e"):
        scratch["chip_full_" + key] = vmem((2, chips, 16, width), bf16)
        for part in ("chip_half_", "chip_others_"):
            scratch[part + key] = vmem((chips, 16, width), bf16)
    for key, rows in (("c", rows_c), ("d", rows_d)):
        for part in ("half_", "quarter_"):
            scratch[part + key] = vmem((4, outers, rows, width), bf16)
        scratch["last_" + key] = vmem((outers, rows, width), bf16)
    for key in ("sem_send", "sem_recv"):
        scratch[key] = pltpu.SemaphoreType.DMA((3, chips))
    names = list(inputs) + list(outputs) + list(scratch)
    spaces = {"items": pltpu.SMEM, "features_far": pl.ANY, "cotangent_far": pl.ANY}
    in_specs = [pl.BlockSpec(memory_space=spaces.get(name, pltpu.VMEM)) for name in inputs]
    whole = pl.BlockSpec(memory_space=pltpu.VMEM)
    made = pl.pallas_call(
        functools.partial(layer_kernel, names, devices),
        out_shape=[jax.ShapeDtypeStruct(*shape) for shape in outputs.values()],
        in_specs=in_specs,
        out_specs=[pl.BlockSpec(memory_space=pl.ANY)] * 2
        + [whole] * 4
        + [pl.BlockSpec(memory_space=pl.ANY)],
        scratch_shapes=list(scratch.values()),
        compiler_params=pltpu.CompilerParams(
            collective_id=0, has_side_effects=True, vmem_limit_bytes=VMEM_BYTES
        ),
    )(*inputs.values())
    flat = list(weights)
    for part in range(9, 12):
        flat[part] = flat[part].reshape(share, LANES)
    shapes = [jax.ShapeDtypeStruct((1, 1), f32)] + [
        jax.ShapeDtypeStruct(flat[index].shape, f32) for index in range(18)
    ]
    order = []
    for index in range(6):
        order += [shapes[1 + 3 * index]] * 3
    updated = pl.pallas_call(
        functools.partial(update_kernel, share),
        out_shape=[jax.ShapeDtypeStruct((points, width), dtype) for dtype in (bf16, f32)]
        + [shapes[0]]
        + order,
        in_specs=[pl.BlockSpec(memory_space=pl.ANY)] * 2
        + [whole] * 4
        + [pl.BlockSpec(memory_space=pl.ANY)] * 18,
        out_specs=[pl.BlockSpec(memory_space=pl.ANY)] * 2 + [whole] * 19,
        scratch_shapes=[
            vmem(square.shape, f32),
            vmem(expand.shape, f32),
            vmem(contract.shape, f32),
            vmem((width, points), bf16),
            vmem((width, points), bf16),
            vmem((points, width), bf16),
            vmem((points, width), f32),
            *(vmem(weight.shape, f32) for weight in flat),
            pltpu.SemaphoreType.DMA((2, 2, PIECES)),
            pltpu.SemaphoreType.DMA((18,)),
        ],
        compiler_params=pltpu.CompilerParams(vmem_limit_bytes=VMEM_BYTES),
    )(*made[:6], *flat)
    layer_output, input_grad, norm, *rest = updated
    for part in range(9, 12):
        rest[part] = rest[part].reshape(fourier.shape)
    return (layer_output, input_grad, norm.reshape(()), *rest)


def shards(features, *others):
    devices = lax.axis_size("pts")
    width = features.shape[1]
    if devices % GROUP == 0 and width == 8 * devices:
        return fused(devices, features, *others)
    return plain(features, *others)


def solution(mesh):
    in_specs = (
        P("pts", None),
        P(None, "pts"),
        P(),
        P("pts"),
        P("pts"),
        P("pts", None),
        P(None, "pts"),
        P(None, "pts"),
        P(None, "pts"),
        P(None, "pts"),
        P(None, "pts"),
        P(None, "pts"),
        P(None, "pts"),
        P(None, "pts"),
        P(None, "pts"),
        P("pts"),
        P("pts"),
        P("pts"),
        P(),
        P(),
        P(),
        P(),
        P(),
        P(),
    )
    out_specs = (
        P("pts", None),
        P("pts", None),
        P(),
        P(None, "pts"),
        P(None, "pts"),
        P(None, "pts"),
        P(None, "pts"),
        P(None, "pts"),
        P(None, "pts"),
        P(None, "pts"),
        P(None, "pts"),
        P(None, "pts"),
        P("pts"),
        P("pts"),
        P("pts"),
        P(),
        P(),
        P(),
        P(),
        P(),
        P(),
    )
    return jax.shard_map(shards, mesh=mesh, in_specs=in_specs, out_specs=out_specs, check_vma=False)
```

profile of v0, /device:TPU:0, one launch (start us, length us, event | category | flops | bytes accessed | tf_op | source)
XLA Modules:
  0.0 142.8 jit_solution(15707531544456488195)
XLA Ops:
  0.7 135.8 %shard_map.391 = (bf16[256,4096]{1,0:T(8,128)(2,1)}, bf16[256,4096]{1,0:T(8,128)(2,1)}, f32[48,256]{1,0:T(8,128)}, f32[64,256]{1,0:T(8,128)}, f32[16,256]{1,0:T(...) custom-call(s32[32]{0:T(128)} %refs_0_.1, bf16[4096,256]{1,0:T(8,128)(2,1)} %refs_1_.1, f32[2,4096]{1,0:T(2,128)} %refs_2_.1, ...), custom_call_target="tpu_custom_call" | custom-call | tf_op jit(solution)/shard_map/pallas_call | solution.py:1622
  136.4 6.2 %shard_map.392 = (bf16[4096,256]{1,0:T(8,128)(2,1)}, f32[4096,256]{1,0:T(8,128)}, f32[1,1]{1,0:T(1,128)}, f32[7,2048]{1,0:T(8,128)}, f32[7,2048]{1,0:T(8,128)}, ...) custom-call(bf16[256,4096]{1,0:T(8,128)(2,1)} %get-tuple-element.48., ...), custom_call_target="tpu_custom_call" | custom-call | tf_op jit(solution)/shard_map/pallas_call | solution.py:1643
where the time goes:
time: 143 us
  Pallas kernels  142 us (99%)
    pallas_call x1, Pallas kernels, fused(): pl.pallas_call(functools.partial(layer_kernel, names, devices), out_shape...  136 us
    pallas_call x1, Pallas kernels, fused(): pl.pallas_call(functools.partial(update_kernel, share), out_shape=[jax.Sh...  6.21 us

commit v1 on v0

--- a/solution.py
+++ b/solution.py
@@ -476,6 +476,11 @@
     return root_inv * (through - centre - scaled * along)
 
 
+def gelu_alone(values):
+    half = 0.5 * values
+    return half + half * jnp.tanh(values * (GELU_C + (GELU_C * GELU_A) * (values * values)))
+
+
 def gelu_both(values):
     square = values * values
     half = 0.5 + 0.5 * jnp.tanh(values * (GELU_C + (GELU_C * GELU_A) * square))
@@ -793,9 +798,14 @@
         barrier, inc=1, device_id=(at.chip * 2 + 1 - at.core,),
         device_id_type=pl.DeviceIdType.MESH,
     )
-    for step in range(1, at.chips):
+    for step in range(1, 4):
         pl.semaphore_signal(
-            barrier, inc=1, device_id=(at.chip_at(step) * 2 + at.core,),
+            barrier, inc=1, device_id=(at.device(at.outer, at.pair_at(step) * 2 + at.core),),
+            device_id_type=pl.DeviceIdType.MESH,
+        )
+    for step in range(1, at.outers):
+        pl.semaphore_signal(
+            barrier, inc=1, device_id=(at.device(at.outer_at(step), at.inner),),
             device_id_type=pl.DeviceIdType.MESH,
         )
 
@@ -871,7 +881,7 @@
     for matrix in range(4):
         pack_square(matrix)
     s.gather_one[at.core, at.pair, at.outer] = low(s.pack[:split, :])
-    pl.semaphore_wait(barrier, at.chips)
+    pl.semaphore_wait(barrier, 4 + at.outers - 1)
     one = Gather(at, s.gather_one, s, (1, 0, 2, 6))
     two = Gather(at, s.gather_two, s, (2, 12, 8, 7))
     one.start_first()
@@ -1111,7 +1121,7 @@
         middle = low(scaled_two * column(2) + column(3))
         s.u2[:, where] = middle
         hidden_pre = dot(s.t_w1[...], middle) + hidden_column(0)
-        hidden = low(gelu(hidden_pre))
+        hidden = low(gelu_alone(hidden_pre))
         s.e1[:, where] = hidden
         s.slope[:, where] = low(hidden_pre)
         encoded = first_sum + dot(s.t_w2[...], hidden) + column(6)
@@ -1201,10 +1211,10 @@
     s.grad_dq[...] = dot_bt(s.phi[...], s.qd[...])
     s.fourier[pl.ds(0, FOUR, stride=2), :] = s.grad_dq[:, :LANES]
     s.fourier[pl.ds(1, FOUR, stride=2), :] = s.grad_dq[:, LANES:]
-    s.grad_do[...] = dot_bt(s.u2[...], s.u3[...])
+    s.grad_o[...] = dot_bt(s.u2[...], s.u3[...])
     table_sum.late(s.table_third)
-    s.grad_p1[...] = dot_bt(s.o[...], s.kv[...])
-    s.grad_p2[...] = dot_bt(s.e1[...], s.u1[...])
+    s.grad_w1[...] = dot_bt(s.o[...], s.kv[...])
+    s.grad_w2[...] = dot_bt(s.e1[...], s.u1[...])
     zeros = jnp.zeros((share, LANES), f32)
 
     def rows_of(chunk, count=1):
@@ -1215,10 +1225,10 @@
         where = rows_of(chunk)
         return jnp.concatenate(
             [
-                s.grad_do[where, :],
-                s.grad_p1[where, :width],
-                s.grad_p1[where, width:],
-                s.grad_p2[rows_of(chunk, 2), :],
+                s.grad_o[where, :],
+                s.grad_w1[where, :width],
+                s.grad_w1[where, width:],
+                s.grad_w2[rows_of(chunk, 2), :],
                 jnp.concatenate([s.fourier[where, :], zeros], axis=1),
             ],
             axis=0,
@@ -1328,12 +1338,12 @@
 
     lax.fori_loop(0, tiles, phase_e, None)
     s.grad_qkv[:, width:] = dot_bt(s.u1[...], s.kv[...])
-    sum_e = ChipSum(at, s, "e")
+    sum_e = ChipSum(at, s, "t")
 
     @pl.loop(0, devices)
     def _(chunk):
         where = rows_of(chunk)
-        s.chip_full_e[lax.rem(chunk, 2), lax.div(chunk, 2)] = low(
+        s.chip_full_t[lax.rem(chunk, 2), lax.div(chunk, 2)] = low(
             jnp.concatenate(
                 [s.grad_qkv[where, width : 2 * width], s.grad_qkv[where, 2 * width :]], axis=0
             )
@@ -1357,9 +1367,10 @@
         s.xh2[:, where] = low(grad_input)
         out_copy(tile, s.xh2, s.input_grad).start()
 
+    sum_e.middle()
+    lax.fori_loop(0, tiles // 2, phase_f, None)
     sum_d.third()
-    sum_e.middle()
-    lax.fori_loop(0, tiles, phase_f, None)
+    lax.fori_loop(tiles // 2, tiles, phase_f, None)
     end_out(s.xh2, s.input_grad)
     s.grads_d[...] = sum_d.finish()
     s.grads_e[...] = sum_e.total()
@@ -1549,11 +1560,8 @@
         "grad_qkv": vmem((width, 3 * width), f32),
         "grad_o": vmem((width, width), f32),
         "grad_kv": vmem((width, 2 * width), f32),
-        "grad_do": vmem((width, width), f32),
         "grad_w1": vmem((width, F), f32),
-        "grad_p1": vmem((width, F), f32),
         "grad_w2": vmem((F, width), f32),
-        "grad_p2": vmem((F, width), f32),
         "grad_dq": vmem((FOUR, width), f32),
         "fourier": vmem((2 * FOUR, LANES), f32),
         "w_qkv": vmem((width, 3 * width), bf16),
@@ -1605,7 +1613,7 @@
         "load_slots": vmem((2, TILE, width), bf16),
         "sem_out": pltpu.SemaphoreType.DMA((points // TILE,)),
     }
-    for key in ("t", "e"):
+    for key in ("t",):
         scratch["chip_full_" + key] = vmem((2, chips, 16, width), bf16)
         for part in ("chip_half_", "chip_others_"):
             scratch[part + key] = vmem((chips, 16, width), bf16)

time: 143 us -> 138 us (0.965)
  Pallas kernels: 142 us -> 137 us
    pallas_call x1, Pallas kernels: 136 us -> 131 us  [fused(): pl.pallas_call(functools.partial(layer_kernel, names, devices), out_shape...]
where the time goes in v1:
time: 138 us
  Pallas kernels  137 us (99%)
    pallas_call x1, Pallas kernels, fused(): pl.pallas_call(functools.partial(layer_kernel, names, devices), out_shape...  131 us
    pallas_call x1, Pallas kernels, fused(): pl.pallas_call(functools.partial(update_kernel, share), out_shape=[jax.Sh...  6.21 us

profile of v1, /device:TPU:0, one launch (start us, length us, event | category | flops | bytes accessed | tf_op | source)
XLA Modules:
  0.0 137.8 jit_solution(5118881655368985619)
XLA Ops:
  0.7 130.7 %shard_map.391 = (bf16[256,4096]{1,0:T(8,128)(2,1)}, bf16[256,4096]{1,0:T(8,128)(2,1)}, f32[48,256]{1,0:T(8,128)}, f32[64,256]{1,0:T(8,128)}, f32[16,256]{1,0:T(...) custom-call(s32[32]{0:T(128)} %refs_0_.1, bf16[4096,256]{1,0:T(8,128)(2,1)} %refs_1_.1, f32[2,4096]{1,0:T(2,128)} %refs_2_.1, ...), custom_call_target="tpu_custom_call" | custom-call | tf_op jit(solution)/shard_map/pallas_call | solution.py:1630
  131.4 6.2 %shard_map.392 = (bf16[4096,256]{1,0:T(8,128)(2,1)}, f32[4096,256]{1,0:T(8,128)}, f32[1,1]{1,0:T(1,128)}, f32[7,2048]{1,0:T(8,128)}, f32[7,2048]{1,0:T(8,128)}, ...) custom-call(bf16[256,4096]{1,0:T(8,128)(2,1)} %get-tuple-element.48., ...), custom_call_target="tpu_custom_call" | custom-call | tf_op jit(solution)/shard_map/pallas_call | solution.py:1651

commit v2 on v1

--- a/solution.py
+++ b/solution.py
@@ -1368,6 +1368,18 @@
         out_copy(tile, s.xh2, s.input_grad).start()
 
     sum_e.middle()
+
+    def gather_sums(indices):
+        lane_wide = lax.broadcasted_iota(jnp.int32, (width, LANES), 1)
+        sums = s.vector_cols[...]
+        for index in indices:
+            sums = jnp.where(
+                lane_wide == index, jnp.sum(s.vector_sum[index], axis=1, keepdims=True), sums
+            )
+        s.vector_cols[...] = sums
+
+    s.vector_cols[...] = jnp.zeros(s.vector_cols.shape, f32)
+    gather_sums(range(2, 12))
     lax.fori_loop(0, tiles // 2, phase_f, None)
     sum_d.third()
     lax.fori_loop(tiles // 2, tiles, phase_f, None)
@@ -1379,13 +1391,7 @@
         for grads in (s.grads_c, s.grads_d, s.grads_e)
     )
 
-    lane_wide = lax.broadcasted_iota(jnp.int32, (width, LANES), 1)
-    sums = jnp.zeros((width, LANES), f32)
-    for index in range(12):
-        sums = jnp.where(
-            lane_wide == index, jnp.sum(s.vector_sum[index], axis=1, keepdims=True), sums
-        )
-    s.vector_cols[...] = sums
+    gather_sums(range(2))
     turned_sums = s.vector_cols[...].T
     high = low(squares).astype(f32)
     s.final_near[at.core] = low(
@@ -1563,7 +1569,7 @@
         "grad_w1": vmem((width, F), f32),
         "grad_w2": vmem((F, width), f32),
         "grad_dq": vmem((FOUR, width), f32),
-        "fourier": vmem((2 * FOUR, LANES), f32),
+        "fourier": vmem((2 * FOUR + 8, LANES), f32),
         "w_qkv": vmem((width, 3 * width), bf16),
         "t_qkv": vmem((3 * width, width), bf16),
         "w_o": vmem((width, width), bf16),

time: 138 us -> 139 us (level)
  no operation moved by 1% of the time
where the time goes in v2:
time: 139 us; the launch traced here: 138 us
  Pallas kernels  137 us (99%)
    pallas_call x1, Pallas kernels, fused(): pl.pallas_call(functools.partial(layer_kernel, names, devices), out_shape...  131 us
    pallas_call x1, Pallas kernels, fused(): pl.pallas_call(functools.partial(update_kernel, share), out_shape=[jax.Sh...  6.21 us

profile of v2, /device:TPU:0, one launch (start us, length us, event | category | flops | bytes accessed | tf_op | source)
XLA Modules:
  0.0 138.3 jit_solution(2693434678636728474)
XLA Ops:
  0.7 131.2 %shard_map.391 = (bf16[256,4096]{1,0:T(8,128)(2,1)}, bf16[256,4096]{1,0:T(8,128)(2,1)}, f32[48,256]{1,0:T(8,128)}, f32[64,256]{1,0:T(8,128)}, f32[16,256]{1,0:T(...) custom-call(s32[32]{0:T(128)} %refs_0_.1, bf16[4096,256]{1,0:T(8,128)(2,1)} %refs_1_.1, f32[2,4096]{1,0:T(2,128)} %refs_2_.1, ...), custom_call_target="tpu_custom_call" | custom-call | tf_op jit(solution)/shard_map/pallas_call | solution.py:1636
  131.9 6.2 %shard_map.392 = (bf16[4096,256]{1,0:T(8,128)(2,1)}, f32[4096,256]{1,0:T(8,128)}, f32[1,1]{1,0:T(1,128)}, f32[7,2048]{1,0:T(8,128)}, f32[7,2048]{1,0:T(8,128)}, ...) custom-call(bf16[256,4096]{1,0:T(8,128)(2,1)} %get-tuple-element.48., ...), custom_call_target="tpu_custom_call" | custom-call | tf_op jit(solution)/shard_map/pallas_call | solution.py:1657
